TPU v7x, 512 devices: a whole 4x8x8 slice. The times are simulated.
512 devices in a mesh: blk: 512 (over y, x, z, core).
Axes of the slice: x: 4, y: 8, z: 8, core: 2. Of those that a mesh axis runs over, the one named last changes fastest.
Arguments:
- pair_density: bfloat16 [196608, 2048], P('blk'), may hold values from -6 to 6
- table: int32 [3, 196608], P(None, 'blk'), may hold values from 0 to 4095, as said below
- gvec: int32 [3, 2048], replicated, may hold values from -8 to 8
- val_energy: float32 [4096, 4], replicated, may hold values from -8 to -0.5
- cond_energy: float32 [4096, 8], replicated, may hold values from 0.5 to 8
Outputs:
- kernel_band: float32 [196608, 1920], P('blk')
Inputs may be any that keep to these rules, and one draw needn't show every extreme that they name: table[0] holds valence bands below 4, table[1] conduction bands below 8, table[2] k-points below 4096.
All inputs are finite; a program needn't handle non-finite values.
Results may differ from a plain program's by a relative error of at most 0.0037.
Values may be sent and summed in bfloat16 or wider, within the bound.
A program may use at most 64 MiB of HBM per device.

v0:
```python
import jax
import jax.numpy as jnp
from jax import lax
from jax.sharding import PartitionSpec as P


def passed_along(block, axis, distance):
    devices = range(lax.axis_size(axis))
    route = [((i - distance) % len(devices), i) for i in devices]
    return lax.ppermute(block, axis, route)


def weighting(gvec):
    shifted = gvec.astype(jnp.float32) + jnp.array([0.1, 0.2, 0.3], jnp.float32)[:, None]
    weight = 1.0 / jnp.sum(shifted * shifted, axis=0)
    return weight / jnp.mean(weight)


def tile_of(left, right, factor):
    product = lax.dot_general(
        left, right, (((1,), (1,)), ((), ())), preferred_element_type=jnp.float32
    )
    return factor * product


def shards(pair_density, table, gvec, val_energy, cond_energy):
    rows = pair_density.shape[0]
    width = pair_density.shape[1]
    norm_weight = weighting(gvec)
    scaled = (pair_density.astype(jnp.float32) * jnp.sqrt(norm_weight)[None, :]).astype(
        jnp.bfloat16
    )
    energy = cond_energy[table[2], table[1]] - val_energy[table[2], table[0]]
    factor = 2.0 / jnp.sqrt(jnp.float32(width))
    nearer = passed_along(scaled, "blk", -1)
    farther = passed_along(nearer, "blk", -1)
    diag_mask = lax.broadcasted_iota(jnp.int32, (rows, rows), 0) == lax.broadcasted_iota(
        jnp.int32, (rows, rows), 1
    )
    own_tile = tile_of(scaled, scaled, factor) + jnp.where(diag_mask, energy[:, None], 0.0)
    upper_one = tile_of(scaled, nearer, factor)
    upper_two = tile_of(scaled, farther, factor)
    lower_one = passed_along(upper_one.T, "blk", 1)
    lower_two = passed_along(upper_two.T, "blk", 2)
    return jnp.concatenate([lower_two, lower_one, own_tile, upper_one, upper_two], axis=1)


def solution(mesh):
    return jax.shard_map(
        shards,
        mesh=mesh,
        in_specs=(P("blk", None), P(None, "blk"), P(), P(), P()),
        out_specs=P("blk", None),
        check_vma=False,
    )
```

profile of v0, /device:TPU:1, one launch (start us, length us, event | category | flops | bytes accessed | tf_op | source)
XLA Modules:
  0.0 98.1 jit_solution(453713035200782321)
XLA Ops:
  0.0 0.0 copy-start
  0.0 0.9 multiply_reduce_fusion
  0.9 0.6 divide_reduce_fusion
  2.2 1.8 %multiply_convert_fusion = bf16[384,2048]{1,0:T(8,128)(2,1)S(1)} fusion(bf16[384,2048]{1,0:T(8,128)(2,1)} %param.6, f32[2048]{0:T(1024)S(1)} %divide_sqrt_fusion), kind=kLoop, calls=%fused_computation.2 | loop fusion | flops 2359296 | bytes 3153920 | tf_op jit(solution)/shard_map/convert_element_type | solution.py:30
  4.0 0.0 copy-start.5
  4.0 8.8 %collective-permute-start = (bf16[384,2048]{1,0:T(8,128)(2,1)S(1)}, bf16[384,2048]{1,0:T(8,128)(2,1)S(1)}, u32[]{:S(2)}, u32[]{:S(2)}) collective-permute-start(bf16[384,2048]{1,0:T(8,128)(2,1)S(1)} %multiply_convert_fusion), channel_id=1, source_target_pairs={{1,0},{2,1},{3,2},{4,3},{5,4},{6,5},{7,6},{8,7},{9,8},{10,9},{11,1... | collective-permute-start | bytes 4718600 | tf_op jit(solution)/shard_map/ppermute | solution.py:10
  12.8 14.7 %collective-permute-done = bf16[384,2048]{1,0:T(8,128)(2,1)S(1)} collective-permute-done((bf16[384,2048]{1,0:T(8,128)(2,1)S(1)}, bf16[384,2048]{1,0:T(8,128)(2,1)S(1)}, u32[]{:S(2)}, u32[]{:S(2)}) %collective-permute-start) | collective-permute-done | bytes 1572896 | tf_op jit(solution)/shard_map/ppermute | solution.py:10
  27.5 13.3 %collective-permute-start.1 = (bf16[384,2048]{1,0:T(8,128)(2,1)S(1)}, bf16[384,2048]{1,0:T(8,128)(2,1)S(1)}, u32[]{:S(2)}, u32[]{:S(2)}) collective-permute-start(bf16[384,2048]{1,0:T(8,128)(2,1)S(1)} %collective-permute-done), channel_id=1, source_target_pairs={{1,0},{2,1},{3,2},{4,3},{5,4},{6,5},{7,6},{8,7},{9,8},{10,9},{11,1... | collective-permute-start | bytes 4718600 | tf_op jit(solution)/shard_map/ppermute | solution.py:10
  40.8 1.0 %convolution_multiply_fusion.1 = f32[384,384]{0,1:T(8,128)S(1)} fusion(bf16[384,2048]{1,0:T(8,128)(2,1)S(1)} %multiply_convert_fusion, bf16[384,2048]{1,0:T(8,128)(2,1)S(1)} %collective-permute-done), kind=kOutput, calls=%fused_computation.6 | convolution fusion | flops 604127232 | bytes 3735552 | tf_op jit(solution)/shard_map/dot_general | solution.py:20
  41.8 0.0 copy-start.6
  41.8 0.0 copy-start.8
  41.8 2.1 %collective-permute-start.3 = (f32[384,384]{1,0:T(8,128)S(1)}, f32[384,384]{1,0:T(8,128)S(1)}, u32[]{:S(2)}, u32[]{:S(2)}) collective-permute-start(f32[384,384]{1,0:T(8,128)S(1)} %bitcast.22), channel_id=1, source_target_pairs={{511,0},{0,1},{1,2},{2,3},{3,4},{4,5},{5,6},{6,7},{7,8},{8,9},{9,1... | collective-permute-start | bytes 1769480 | tf_op jit(solution)/shard_map/ppermute | solution.py:10
  43.9 5.3 %collective-permute-done.1 = bf16[384,2048]{1,0:T(8,128)(2,1)S(1)} collective-permute-done((bf16[384,2048]{1,0:T(8,128)(2,1)S(1)}, bf16[384,2048]{1,0:T(8,128)(2,1)S(1)}, u32[]{:S(2)}, u32[]{:S(2)}) %collective-permute-start.1) | collective-permute-done | bytes 1572896 | tf_op jit(solution)/shard_map/ppermute | solution.py:10
  49.2 0.0 copy-done.5
  49.2 1.0 %convolution_multiply_fusion.2 = f32[384,384]{0,1:T(8,128)S(1)} fusion(bf16[384,2048]{1,0:T(8,128)(2,1)S(1)} %multiply_convert_fusion, bf16[384,2048]{1,0:T(8,128)(2,1)S(1)} %collective-permute-done.1), kind=kOutput, calls=%fused_computation.7 | convolution fusion | flops 604127232 | bytes 3735552 | tf_op jit(solution)/shard_map/dot_general | solution.py:20
  50.2 0.0 copy-done.6
  50.2 0.0 copy-start.2
  50.2 0.0 copy-start.1
  50.2 0.2 copy.10
  50.5 0.6 copy-done.2
  51.0 4.3 %collective-permute-start.2 = (f32[384,384]{0,1:T(8,128)S(1)}, f32[384,384]{0,1:T(8,128)}, u32[]{:S(2)}, u32[]{:S(2)}) collective-permute-start(f32[384,384]{0,1:T(8,128)S(1)} %bitcast.23), channel_id=1, source_target_pairs={{510,0},{511,1},{0,2},{1,3},{2,4},{3,5},{4,6},{5,7},{6,8},{7,9},{8... | collective-permute-start | bytes 1769480 | tf_op jit(solution)/shard_map/ppermute | solution.py:10
  55.3 0.0 copy-done.8
  55.4 0.0 copy-done
  55.4 2.7 %gather_fusion = f32[384]{0:T(512)S(1)} fusion(f32[4096,8]{0,1:T(8,128)S(1)} %copy-done, s32[384]{0:T(512)S(1)} %get-tuple-element.6), kind=kCustom, calls=%fused_computation | custom fusion | bytes 6144 | tf_op jit(solution)/shard_map/gather | solution.py:33
  58.1 0.0 copy-done.1
  58.1 3.7 %gather_fusion.1 = f32[384]{0:T(512)S(1)} fusion(f32[4096,4]{0,1:T(4,128)S(1)} %copy-done.1, s32[384]{0:T(512)S(1)} %get-tuple-element.5), kind=kCustom, calls=%fused_computation.1 | custom fusion | bytes 6144 | tf_op jit(solution)/shard_map/gather | solution.py:33
  61.8 0.0 collective-permute-done.3
  61.8 1.1 %copy.11 = f32[384,384]{0,1:T(8,128)} copy(f32[384,384]{1,0:T(8,128)S(1)} %collective-permute-done.3) | data formatting | bytes 1179648 | tf_op jit(solution)/shard_map/ppermute | solution.py:10
  62.9 0.0 copy-start.4
  62.9 27.5 %collective-permute-done.2 = f32[384,384]{0,1:T(8,128)} collective-permute-done((f32[384,384]{0,1:T(8,128)S(1)}, f32[384,384]{0,1:T(8,128)}, u32[]{:S(2)}, u32[]{:S(2)}) %collective-permute-start.2) | collective-permute-done | bytes 589856 | tf_op jit(solution)/shard_map/ppermute | solution.py:10
  90.4 1.1 %constant_dynamic-update-slice_fusion.3 = f32[384,1920]{0,1:T(8,128)S(1)} fusion(f32[384,384]{0,1:T(8,128)} %collective-permute-done.2), kind=kLoop, calls=%fused_computation.13 | loop fusion | bytes 1179648
  91.5 0.0 copy-done.4
  91.6 0.0 copy-start.7
  91.6 2.9 %fusion.1 = f32[384,1920]{0,1:T(8,128)S(1)} fusion(f32[384,1920]{0,1:T(8,128)S(1)} %constant_dynamic-update-slice_fusion.2, bf16[384,2048]{1,0:T(8,128)(2,1)} %copy-done.5, f32[384]{0:T(512)S(1)} %sub.7), kind=kOutput, calls=%fused_computation.5 | convolution fusion | flops 604569600 | bytes 3737600 | tf_op jit(solution)/shard_map/dot_general | solution.py:20
  94.5 0.0 copy-done.7
  94.5 0.0 copy-start.3
  94.6 1.0 %copy-done.3 = f32[384,384]{0,1:T(8,128)S(1)} copy-done((f32[384,384]{0,1:T(8,128)S(1)}, f32[384,384]{0,1:T(8,128)}, u32[]{:S(2)}) %copy-start.3) | copy-done | bytes 589848
  95.6 2.4 %copy.12 = f32[384,1920]{1,0:T(8,128)} copy(f32[384,1920]{0,1:T(8,128)S(1)} %constant_dynamic-update-slice_fusion) | data formatting | bytes 5898240 | tf_op jit(solution)/shard_map/concatenate | solution.py:45
  (6 shorter events, 0.2 us)
Async XLA Ops:
  0.0 55.4 %copy-start = (f32[4096,8]{0,1:T(8,128)S(1)}, f32[4096,8]{0,1:T(8,128)}, u32[]{:S(2)}) copy-start(f32[4096,8]{0,1:T(8,128)} %param.10) | copy-start | bytes 393220
  4.0 45.2 %copy-start.5 = (bf16[384,2048]{1,0:T(8,128)(2,1)}, bf16[384,2048]{1,0:T(8,128)(2,1)S(1)}, u32[]{:S(2)}) copy-start(bf16[384,2048]{1,0:T(8,128)(2,1)S(1)} %multiply_convert_fusion) | copy-start | bytes 4718596
  4.0 23.5 %collective-permute-start = (bf16[384,2048]{1,0:T(8,128)(2,1)S(1)}, bf16[384,2048]{1,0:T(8,128)(2,1)S(1)}, u32[]{:S(2)}, u32[]{:S(2)}) collective-permute-start(bf16[384,2048]{1,0:T(8,128)(2,1)S(1)} %multiply_convert_fusion), channel_id=1, source_target_pairs={{1,0},{2,1},{3,2},{4,3},{5,4},{6,5},{7,6},{8,7},{9,8},{10,9},{11,1... | collective-permute-start | bytes 4718600 | tf_op jit(solution)/shard_map/ppermute | solution.py:10
  27.5 21.7 %collective-permute-start.1 = (bf16[384,2048]{1,0:T(8,128)(2,1)S(1)}, bf16[384,2048]{1,0:T(8,128)(2,1)S(1)}, u32[]{:S(2)}, u32[]{:S(2)}) collective-permute-start(bf16[384,2048]{1,0:T(8,128)(2,1)S(1)} %collective-permute-done), channel_id=1, source_target_pairs={{1,0},{2,1},{3,2},{4,3},{5,4},{6,5},{7,6},{8,7},{9,8},{10,9},{11,1... | collective-permute-start | bytes 4718600 | tf_op jit(solution)/shard_map/ppermute | solution.py:10
  41.8 8.4 %copy-start.6 = (f32[384,384]{0,1:T(8,128)}, f32[384,384]{0,1:T(8,128)S(1)}, u32[]{:S(2)}) copy-start(f32[384,384]{0,1:T(8,128)S(1)} %convolution_multiply_fusion.1) | copy-start | bytes 1769476
  41.8 13.5 %copy-start.8 = (s32[3,384]{1,0:T(4,128)S(1)}, s32[3,384]{1,0:T(4,128)}, u32[]{:S(2)}) copy-start(s32[3,384]{1,0:T(4,128)} %param.7) | copy-start | bytes 13828
  41.8 19.9 %collective-permute-start.3 = (f32[384,384]{1,0:T(8,128)S(1)}, f32[384,384]{1,0:T(8,128)S(1)}, u32[]{:S(2)}, u32[]{:S(2)}) collective-permute-start(f32[384,384]{1,0:T(8,128)S(1)} %bitcast.22), channel_id=1, source_target_pairs={{511,0},{0,1},{1,2},{2,3},{3,4},{4,5},{5,6},{6,7},{7,8},{8,9},{9,1... | collective-permute-start | bytes 1769480 | tf_op jit(solution)/shard_map/ppermute | solution.py:10
  50.2 0.8 copy-start.2
  50.2 7.8 %copy-start.1 = (f32[4096,4]{0,1:T(4,128)S(1)}, f32[4096,4]{0,1:T(4,128)}, u32[]{:S(2)}) copy-start(f32[4096,4]{0,1:T(4,128)} %param.9) | copy-start | bytes 196612
  51.0 39.4 %collective-permute-start.2 = (f32[384,384]{0,1:T(8,128)S(1)}, f32[384,384]{0,1:T(8,128)}, u32[]{:S(2)}, u32[]{:S(2)}) collective-permute-start(f32[384,384]{0,1:T(8,128)S(1)} %bitcast.23), channel_id=1, source_target_pairs={{510,0},{511,1},{0,2},{1,3},{2,4},{3,5},{4,6},{5,7},{6,8},{7,9},{8... | collective-permute-start | bytes 1769480 | tf_op jit(solution)/shard_map/ppermute | solution.py:10
  62.9 28.7 %copy-start.4 = (f32[384,384]{0,1:T(8,128)S(1)}, f32[384,384]{0,1:T(8,128)}, u32[]{:S(2)}) copy-start(f32[384,384]{0,1:T(8,128)} %copy.11) | copy-start | bytes 1769476
  91.6 3.0 %copy-start.7 = (f32[384,384]{0,1:T(8,128)S(1)}, f32[384,384]{0,1:T(8,128)}, u32[]{:S(2)}) copy-start(f32[384,384]{0,1:T(8,128)} %copy-done.6) | copy-start | bytes 1769476
  94.5 1.1 %copy-start.3 = (f32[384,384]{0,1:T(8,128)S(1)}, f32[384,384]{0,1:T(8,128)}, u32[]{:S(2)}) copy-start(f32[384,384]{0,1:T(8,128)} %copy-done.2) | copy-start | bytes 1769476
where the time goes:
time: 98.5 us; the launch traced here: 98.1 us
  waiting for transfers between devices  47.5 us (48%)
  starting transfers between devices  28.5 us (29%)
  local copies, waits for them, and re-layouts  12.9 us (13%)
  matrix products  4.96 us (5%)
  other arithmetic  3.33 us (3%)
    ppermute x4, waiting for transfers between devices, passed_along(): return lax.ppermute(block, axis, route)  47.5 us
    ppermute x4, starting transfers between devices, passed_along(): return lax.ppermute(block, axis, route)  28.5 us
    gather x2, local copies, waits for them, and re-layouts, shards(): energy = cond_energy[table[2], table[1]] - val_energy[table[2], table[0]]  6.36 us
    dot_general x3, matrix products, tile_of(): lax.dot_general(left, right, (((1,), (1,)), ((), ())), preferred_element_...  4.96 us
    unnamed x21, local copies, waits for them, and re-layouts  2.78 us
    concatenate x2, local copies, waits for them, and re-layouts, shards(): jnp.concatenate([lower_two, lower_one, own_tile, upper_one, upper_two], a...  2.45 us
  transfers between devices with their start and end apart: 4, of which 3 were waited for; matrix products, arithmetic and copies ran while one was open for 10% of the time, Pallas kernels for 0%

commit v1 on v0

v1 whole, which is shorter than its diff:
```python
import functools

import jax
import jax.numpy as jnp
from jax import lax
from jax.experimental import pallas as pl
from jax.experimental.pallas import tpu as pltpu
from jax.sharding import PartitionSpec as P

MESH = pl.DeviceIdType.MESH
CHUNK = 128
KSTEP = 512
SCALE_ROWS = 32


def times_transposed(left, right):
    return lax.dot_general(
        left, right, (((1,), (1,)), ((), ())), preferred_element_type=jnp.float32
    )


def picked(values, matches):
    high = values.astype(jnp.bfloat16)
    rest = values - high.astype(jnp.float32)
    middle = rest.astype(jnp.bfloat16)
    low = (rest - middle.astype(jnp.float32)).astype(jnp.bfloat16)
    dot = functools.partial(jnp.dot, preferred_element_type=jnp.float32)
    return dot(high, matches) + dot(middle, matches) + dot(low, matches)


def kernel(
    n, x_ref, table_ref, gvec_ref, val_ref, cond_ref, out_ref,
    both, other, far, far_out, far_in, table, gvec, val, cond, weight, energy,
    local_sem, sib_sem, block_sem, side_sem, back_sem,
):
    rows, width = x_ref.shape
    chunks = rows // CHUNK
    me = lax.axis_index("blk")
    core = lax.rem(me, 2)
    sib = me + 1 - 2 * core
    out = lax.rem(me + n - 1 + 2 * core, n)
    at_own = 2 * rows
    at_sib = pl.multiple_of((3 - 2 * core) * rows, 128)
    at_out = pl.multiple_of((1 + 2 * core) * rows, 128)
    at_far = pl.multiple_of((4 * core) * rows, 128)
    at_side = pl.multiple_of((4 * core) * rows, 128)

    def remote(src, dst, sems, i, device):
        return pltpu.make_async_remote_copy(
            src_ref=src, dst_ref=dst, send_sem=sems.at[0, i], recv_sem=sems.at[1, i],
            device_id=(device,), device_id_type=MESH,
        )

    barrier = pltpu.get_barrier_semaphore()
    for peer in (out, sib):
        pl.semaphore_signal(barrier, inc=1, device_id=(peer,), device_id_type=MESH)

    locals_ = [
        pltpu.make_async_copy(src, dst, local_sem.at[i])
        for i, (src, dst) in enumerate(
            [
                (gvec_ref, gvec),
                (x_ref, both.at[pl.ds(0, rows)]),
                (table_ref, table),
                (val_ref, val),
                (cond_ref, cond),
            ]
        )
    ]
    for copy in locals_:
        copy.start()
    pl.semaphore_wait(barrier, 2)

    blocks = []
    for i in range(chunks):
        part = pl.ds(i * CHUNK, CHUNK)
        blocks.append(remote(x_ref.at[part], other.at[part], block_sem, i, out))
        blocks[-1].start()
    beside = remote(x_ref, both.at[pl.ds(rows, rows)], sib_sem, 0, sib)
    beside.start()

    locals_[0].wait()
    total = jnp.zeros((1, width), jnp.float32)
    for axis, shift in enumerate((0.1, 0.2, 0.3)):
        component = gvec[axis : axis + 1, :].astype(jnp.float32) + jnp.float32(shift)
        total = total + component * component
    inverse = 1.0 / total
    weight[...] = jnp.sqrt(inverse / jnp.mean(inverse))

    def scale(ref, first, count):
        def body(step, carry):
            part = pl.ds(pl.multiple_of(first + step * SCALE_ROWS, SCALE_ROWS), SCALE_ROWS)
            ref[part, :] = (ref[part, :].astype(jnp.float32) * weight[...]).astype(jnp.bfloat16)
            return carry

        lax.fori_loop(0, count // SCALE_ROWS, body, 0)

    factor = 2.0 / jnp.sqrt(jnp.full((1, 1), width, jnp.float32))

    for copy in locals_[2:]:
        copy.wait()
    nk = cond.shape[1]
    k_row = table[2:3, :]

    def match(step, carry):
        of_val, of_cond = carry
        first = pl.multiple_of(step * KSTEP, KSTEP)
        numbers = lax.broadcasted_iota(jnp.int32, (KSTEP, rows), 0) + first
        matches = (numbers == k_row).astype(jnp.float32).astype(jnp.bfloat16)
        part = pl.ds(first, KSTEP)
        return of_val + picked(val[:, part], matches), of_cond + picked(cond[:, part], matches)

    of_val, of_cond = lax.fori_loop(
        0, nk // KSTEP, match,
        (jnp.zeros((val.shape[0], rows), jnp.float32), jnp.zeros((cond.shape[0], rows), jnp.float32)),
    )

    def band(values, chosen):
        bands = lax.broadcasted_iota(jnp.int32, values.shape, 0)
        return jnp.sum(jnp.where(bands == chosen, values, 0.0), axis=0, keepdims=True)

    energy[...] = band(of_cond, table[1:2, :]) - band(of_val, table[0:1, :])

    locals_[1].wait()
    scale(both, 0, rows)

    def own(step, carry):
        first = pl.multiple_of(step * CHUNK, CHUNK)
        part = pl.ds(first, CHUNK)
        tile = factor * times_transposed(both[part, :], both[pl.ds(0, rows), :])
        i = lax.broadcasted_iota(jnp.int32, tile.shape, 0) + first
        j = lax.broadcasted_iota(jnp.int32, tile.shape, 1)
        out_ref[part, pl.ds(at_own, rows)] = tile + jnp.where(i == j, energy[...], 0.0)
        return carry

    lax.fori_loop(0, chunks, own, 0)

    beside.wait_recv()
    scale(both, rows, rows)

    def near(step, carry):
        part = pl.ds(pl.multiple_of(step * CHUNK, CHUNK), CHUNK)
        out_ref[part, pl.ds(at_sib, rows)] = factor * times_transposed(
            both[part, :], both[pl.ds(rows, rows), :]
        )
        return carry

    lax.fori_loop(0, chunks, near, 0)

    sides, backs = [], []
    for i in range(chunks):
        first = i * CHUNK
        part = pl.ds(first, CHUNK)
        blocks[i].wait_recv()
        scale(other, first, CHUNK)
        far_out[part, :] = (
            factor * times_transposed(other[part, :], both[pl.ds(rows, rows), :])
        ).astype(jnp.bfloat16)
        backs.append(remote(far_out.at[part], far_in.at[part], back_sem, i, out))
        backs[-1].start()
        far[i] = factor * times_transposed(both[pl.ds(rows, rows), :], other[part, :])
        sides.append(
            remote(
                far.at[i],
                out_ref.at[:, pl.ds(pl.multiple_of(at_side + first, 128), CHUNK)],
                side_sem, i, sib,
            )
        )
        sides[-1].start()
        out_ref[:, pl.ds(pl.multiple_of(at_out + first, 128), CHUNK)] = factor * times_transposed(
            both[pl.ds(0, rows), :], other[part, :]
        )

    for i in range(chunks):
        part = pl.ds(i * CHUNK, CHUNK)
        backs[i].wait_recv()
        out_ref[part, pl.ds(at_far, rows)] = far_in[part, :].astype(jnp.float32)
    for copy in sides:
        copy.wait()
    for copy in blocks + backs + [beside]:
        copy.wait_send()


def shards(pair_density, table, gvec, val_energy, cond_energy):
    rows, width = pair_density.shape
    n = lax.axis_size("blk")
    nk, nv = val_energy.shape
    nc = cond_energy.shape[1]
    chunks = rows // CHUNK
    anywhere = pl.BlockSpec(memory_space=pltpu.HBM)
    return pl.pallas_call(
        functools.partial(kernel, n),
        out_shape=jax.ShapeDtypeStruct((rows, 5 * rows), jnp.float32),
        in_specs=[anywhere] * 5,
        out_specs=pl.BlockSpec(memory_space=pltpu.VMEM),
        scratch_shapes=[
            pltpu.VMEM((2 * rows, width), jnp.bfloat16),
            pltpu.VMEM((rows, width), jnp.bfloat16),
            pltpu.VMEM((chunks, rows, CHUNK), jnp.float32),
            pltpu.VMEM((rows, rows), jnp.bfloat16),
            pltpu.VMEM((rows, rows), jnp.bfloat16),
            pltpu.VMEM((3, rows), jnp.int32),
            pltpu.VMEM((3, width), jnp.int32),
            pltpu.VMEM((nv, nk), jnp.float32),
            pltpu.VMEM((nc, nk), jnp.float32),
            pltpu.VMEM((1, width), jnp.float32),
            pltpu.VMEM((1, rows), jnp.float32),
            pltpu.SemaphoreType.DMA((5,)),
            pltpu.SemaphoreType.DMA((2, 1)),
            pltpu.SemaphoreType.DMA((2, chunks)),
            pltpu.SemaphoreType.DMA((2, chunks)),
            pltpu.SemaphoreType.DMA((2, chunks)),
        ],
        compiler_params=pltpu.CompilerParams(
            collective_id=0, has_side_effects=True, vmem_limit_bytes=32 << 20
        ),
        name="band",
    )(*[pltpu.with_memory_space_constraint(v, pltpu.HBM) for v in (pair_density, table, gvec, val_energy.T, cond_energy.T)])


def solution(mesh):
    return jax.shard_map(
        shards,
        mesh=mesh,
        in_specs=(P("blk", None), P(None, "blk"), P(), P(), P()),
        out_specs=P("blk", None),
        check_vma=False,
    )
```

time: 98.5 us -> 41.8 us (0.42)
  the two profiles are of different devices: /device:TPU:1 before, /device:TPU:56 now
where the time goes in v1:
time: 41.8 us; the launch traced here: 41.4 us
  Pallas kernels  39.8 us (95%)
  local copies, waits for them, and re-layouts  1.6 us (4%)
    pallas_call x1, Pallas kernels, shards(): pl.pallas_call(functools.partial(kernel, n), out_shape=jax.ShapeDtypeStru...  39.8 us
    unnamed x1, local copies, waits for them, and re-layouts  1.6 us

profile of v1, /device:TPU:56, one launch (start us, length us, event | category | flops | bytes accessed | tf_op | source)
XLA Modules:
  0.0 41.4 jit_solution(8647464451076793023)
XLA Ops:
  0.0 39.8 %band.1 = f32[384,1920]{1,0:T(8,128)S(1)} custom-call(bf16[384,2048]{1,0:T(8,128)(2,1)} %x_ref.1, s32[3,384]{1,0:T(4,128)} %table_ref.1, s32[3,2048]{1,0:T(4,128)} %gvec_ref.1, f32[4,4096]{1,0:T(4,128)} %bitcast.3, f32[8,4096]{1,0:T(8,128)} %bitcast.2), custom_call_target="tpu_custom_call" | custom-call | tf_op jit(solution)/shard_map/band/pallas_call | solution.py:191
  39.8 1.6 %copy.7 = f32[384,1920]{1,0:T(8,128)} copy(f32[384,1920]{1,0:T(8,128)S(1)} %band.1) | data formatting | bytes 5898240

commit v2 on v1

--- a/solution.py
+++ b/solution.py
@@ -9,6 +9,9 @@
 
 MESH = pl.DeviceIdType.MESH
 CHUNK = 128
+PIECES = (64, 64, 64, 64, 64, 32, 32)
+FOOT_WAITS = 3
+COLUMN = 8
 KSTEP = 512
 SCALE_ROWS = 32
 
@@ -19,41 +22,62 @@
     )
 
 
-def picked(values, matches):
-    high = values.astype(jnp.bfloat16)
-    rest = values - high.astype(jnp.float32)
-    middle = rest.astype(jnp.bfloat16)
-    low = (rest - middle.astype(jnp.float32)).astype(jnp.bfloat16)
-    dot = functools.partial(jnp.dot, preferred_element_type=jnp.float32)
-    return dot(high, matches) + dot(middle, matches) + dot(low, matches)
+def in_three(values):
+    high = values.astype(jnp.bfloat16).astype(jnp.float32)
+    rest = values - high
+    middle = rest.astype(jnp.bfloat16).astype(jnp.float32)
+    return [high, middle, rest - middle]
 
 
 def kernel(
     n, x_ref, table_ref, gvec_ref, val_ref, cond_ref, out_ref,
-    both, other, far, far_out, far_in, table, gvec, val, cond, weight, energy,
-    local_sem, sib_sem, block_sem, side_sem, back_sem,
+    both, other, relay, far, far_out, far_in, table, gvec, val, cond, terms, weight, energy,
+    local_sem, sib_sem, block_sem, relay_sem, side_sem, back_sem, helper_ready, foot_ready,
 ):
     rows, width = x_ref.shape
     chunks = rows // CHUNK
+    parts, first = [], 0
+    for size in PIECES:
+        parts.append(pl.ds(first, size))
+        first += size
     me = lax.axis_index("blk")
     core = lax.rem(me, 2)
+    level = lax.rem(me // 2, COLUMN)
     sib = me + 1 - 2 * core
     out = lax.rem(me + n - 1 + 2 * core, n)
+    foot = jnp.logical_and(level == 0, core == 0)
+    helper = jnp.logical_and(level == 0, core == 1)
+    top = jnp.logical_and(level == COLUMN - 1, core == 1)
+    my_helper = lax.rem(me + n - 2 * COLUMN + 1, n)
+    helped_foot = lax.rem(me + 2 * COLUMN - 1, n)
+    helped_top = lax.rem(me + 2 * COLUMN - 2, n)
+    top_helper = lax.rem(me + n - 2 * COLUMN + 2, n)
     at_own = 2 * rows
     at_sib = pl.multiple_of((3 - 2 * core) * rows, 128)
     at_out = pl.multiple_of((1 + 2 * core) * rows, 128)
     at_far = pl.multiple_of((4 * core) * rows, 128)
     at_side = pl.multiple_of((4 * core) * rows, 128)
 
-    def remote(src, dst, sems, i, device):
+    def remote(src, dst, send_sem, recv_sem, device):
         return pltpu.make_async_remote_copy(
-            src_ref=src, dst_ref=dst, send_sem=sems.at[0, i], recv_sem=sems.at[1, i],
+            src_ref=src, dst_ref=dst, send_sem=send_sem, recv_sem=recv_sem,
             device_id=(device,), device_id_type=MESH,
         )
 
+    def signal(sem, device):
+        pl.semaphore_signal(sem, inc=1, device_id=(device,), device_id_type=MESH)
+
     barrier = pltpu.get_barrier_semaphore()
-    for peer in (out, sib):
-        pl.semaphore_signal(barrier, inc=1, device_id=(peer,), device_id_type=MESH)
+    signal(barrier, sib)
+
+    @pl.when(jnp.logical_not(top))
+    def _():
+        signal(barrier, out)
+
+    @pl.when(helper)
+    def _():
+        signal(barrier, helped_foot)
+        signal(barrier, helped_top)
 
     locals_ = [
         pltpu.make_async_copy(src, dst, local_sem.at[i])
@@ -69,15 +93,46 @@
     ]
     for copy in locals_:
         copy.start()
-    pl.semaphore_wait(barrier, 2)
-
-    blocks = []
-    for i in range(chunks):
-        part = pl.ds(i * CHUNK, CHUNK)
-        blocks.append(remote(x_ref.at[part], other.at[part], block_sem, i, out))
-        blocks[-1].start()
-    beside = remote(x_ref, both.at[pl.ds(rows, rows)], sib_sem, 0, sib)
+    pl.semaphore_wait(barrier, jnp.where(top, 3, 2))
+
+    blocks = [
+        remote(x_ref.at[part], other.at[part], block_sem.at[0, i], block_sem.at[1, i], out)
+        for i, part in enumerate(parts)
+    ]
+    passes = [
+        remote(x_ref.at[part], relay.at[part], block_sem.at[0, i], relay_sem.at[1, i], my_helper)
+        for i, part in enumerate(parts)
+    ]
+
+    @pl.when(top)
+    def _():
+        signal(helper_ready, top_helper)
+        signal(foot_ready, out)
+
+    beside = remote(x_ref, both.at[pl.ds(rows, rows)], sib_sem.at[0], sib_sem.at[1], sib)
+
+    @pl.when(foot)
+    def _():
+        for copy in passes:
+            copy.start()
+
+    @pl.when(jnp.logical_not(foot))
+    def _():
+        for copy in blocks:
+            copy.start()
+
     beside.start()
+
+    onward = [
+        remote(relay.at[part], other.at[part], relay_sem.at[0, i], block_sem.at[1, i], helped_top)
+        for i, part in enumerate(parts)
+    ]
+
+    def hand_on(i):
+        @pl.when(helper)
+        def _():
+            passes[i].wait_recv()
+            onward[i].start()
 
     locals_[0].wait()
     total = jnp.zeros((1, width), jnp.float32)
@@ -99,21 +154,22 @@
 
     for copy in locals_[2:]:
         copy.wait()
-    nk = cond.shape[1]
+    nk, nv = val.shape[1], val.shape[0]
+    padded = jnp.concatenate([val[...], jnp.zeros((8 - nv, nk), jnp.float32)], axis=0)
+    terms[...] = jnp.concatenate(in_three(cond[...]) + in_three(padded), axis=0).astype(jnp.bfloat16)
     k_row = table[2:3, :]
 
     def match(step, carry):
-        of_val, of_cond = carry
         first = pl.multiple_of(step * KSTEP, KSTEP)
         numbers = lax.broadcasted_iota(jnp.int32, (KSTEP, rows), 0) + first
         matches = (numbers == k_row).astype(jnp.float32).astype(jnp.bfloat16)
-        part = pl.ds(first, KSTEP)
-        return of_val + picked(val[:, part], matches), of_cond + picked(cond[:, part], matches)
-
-    of_val, of_cond = lax.fori_loop(
-        0, nk // KSTEP, match,
-        (jnp.zeros((val.shape[0], rows), jnp.float32), jnp.zeros((cond.shape[0], rows), jnp.float32)),
-    )
+        return carry + jnp.dot(
+            terms[:, pl.ds(first, KSTEP)], matches, preferred_element_type=jnp.float32
+        )
+
+    picked = lax.fori_loop(0, nk // KSTEP, match, jnp.zeros((48, rows), jnp.float32))
+    of_cond = picked[0:8, :] + picked[8:16, :] + picked[16:24, :]
+    of_val = picked[24:32, :] + picked[32:40, :] + picked[40:48, :]
 
     def band(values, chosen):
         bands = lax.broadcasted_iota(jnp.int32, values.shape, 0)
@@ -147,38 +203,67 @@
 
     lax.fori_loop(0, chunks, near, 0)
 
-    sides, backs = [], []
-    for i in range(chunks):
-        first = i * CHUNK
-        part = pl.ds(first, CHUNK)
+    @pl.when(helper)
+    def _():
+        pl.semaphore_wait(helper_ready, 1)
+
+    @pl.when(foot)
+    def _():
+        pl.semaphore_wait(foot_ready, 1)
+
+    hand_on(0)
+
+    sides, backs, group_rows = [], [], []
+    for i, part in enumerate(parts):
         blocks[i].wait_recv()
-        scale(other, first, CHUNK)
-        far_out[part, :] = (
-            factor * times_transposed(other[part, :], both[pl.ds(rows, rows), :])
-        ).astype(jnp.bfloat16)
-        backs.append(remote(far_out.at[part], far_in.at[part], back_sem, i, out))
-        backs[-1].start()
-        far[i] = factor * times_transposed(both[pl.ds(rows, rows), :], other[part, :])
+        scale(other, part.start, part.size)
+        product = factor * times_transposed(other[part, :], both[pl.ds(rows, rows), :])
+        far_out[part, :] = product.astype(jnp.bfloat16)
+        group_rows.append(product)
+        backs.append(
+            remote(far_out.at[part], far_in.at[part], back_sem.at[0, i], back_sem.at[1, i], out)
+        )
+        pl.when(jnp.logical_not(foot))(backs[-1].start)
+        if i + 1 < len(parts):
+            hand_on(i + 1)
+        end = part.start + part.size
+        if end % CHUNK:
+            continue
+        group = end // CHUNK - 1
+        chunk = pl.ds(end - CHUNK, CHUNK)
+        far[group] = jnp.concatenate(group_rows, axis=0).T
+        group_rows.clear()
         sides.append(
             remote(
-                far.at[i],
-                out_ref.at[:, pl.ds(pl.multiple_of(at_side + first, 128), CHUNK)],
-                side_sem, i, sib,
+                far.at[group],
+                out_ref.at[:, pl.ds(pl.multiple_of(at_side + end - CHUNK, 128), CHUNK)],
+                side_sem.at[0, group], side_sem.at[1, group], sib,
             )
         )
         sides[-1].start()
-        out_ref[:, pl.ds(pl.multiple_of(at_out + first, 128), CHUNK)] = factor * times_transposed(
-            both[pl.ds(0, rows), :], other[part, :]
-        )
-
-    for i in range(chunks):
-        part = pl.ds(i * CHUNK, CHUNK)
+        out_ref[:, pl.ds(pl.multiple_of(at_out + end - CHUNK, 128), CHUNK)] = (
+            factor * times_transposed(both[pl.ds(0, rows), :], other[chunk, :])
+        )
+
+    for i, part in enumerate(parts):
         backs[i].wait_recv()
         out_ref[part, pl.ds(at_far, rows)] = far_in[part, :].astype(jnp.float32)
+        if i == FOOT_WAITS:
+
+            @pl.when(foot)
+            def _():
+                for copy in backs:
+                    copy.start()
+
     for copy in sides:
         copy.wait()
     for copy in blocks + backs + [beside]:
         copy.wait_send()
+
+    @pl.when(helper)
+    def _():
+        for copy in onward:
+            copy.wait_send()
 
 
 def shards(pair_density, table, gvec, val_energy, cond_energy):
@@ -196,6 +281,7 @@
         scratch_shapes=[
             pltpu.VMEM((2 * rows, width), jnp.bfloat16),
             pltpu.VMEM((rows, width), jnp.bfloat16),
+            pltpu.VMEM((rows, width), jnp.bfloat16),
             pltpu.VMEM((chunks, rows, CHUNK), jnp.float32),
             pltpu.VMEM((rows, rows), jnp.bfloat16),
             pltpu.VMEM((rows, rows), jnp.bfloat16),
@@ -203,13 +289,17 @@
             pltpu.VMEM((3, width), jnp.int32),
             pltpu.VMEM((nv, nk), jnp.float32),
             pltpu.VMEM((nc, nk), jnp.float32),
+            pltpu.VMEM((48, nk), jnp.bfloat16),
             pltpu.VMEM((1, width), jnp.float32),
             pltpu.VMEM((1, rows), jnp.float32),
             pltpu.SemaphoreType.DMA((5,)),
-            pltpu.SemaphoreType.DMA((2, 1)),
+            pltpu.SemaphoreType.DMA((2,)),
+            pltpu.SemaphoreType.DMA((2, len(PIECES))),
+            pltpu.SemaphoreType.DMA((2, len(PIECES))),
             pltpu.SemaphoreType.DMA((2, chunks)),
-            pltpu.SemaphoreType.DMA((2, chunks)),
-            pltpu.SemaphoreType.DMA((2, chunks)),
+            pltpu.SemaphoreType.DMA((2, len(PIECES))),
+            pltpu.SemaphoreType.REGULAR,
+            pltpu.SemaphoreType.REGULAR,
         ],
         compiler_params=pltpu.CompilerParams(
             collective_id=0, has_side_effects=True, vmem_limit_bytes=32 << 20

time: 41.8 us -> 39.8 us (0.952)
  Pallas kernels: 39.8 us -> 38 us
    pallas_call x1, Pallas kernels: 39.8 us -> 38 us  [shards(): pl.pallas_call(functools.partial(kernel, n), out_shape=jax.ShapeDtypeStru...]
where the time goes in v2:
time: 39.8 us; the launch traced here: 39.6 us
  Pallas kernels  38 us (95%)
  local copies, waits for them, and re-layouts  1.6 us (4%)
    pallas_call x1, Pallas kernels, shards(): pl.pallas_call(functools.partial(kernel, n), out_shape=jax.ShapeDtypeStru...  38 us
    unnamed x1, local copies, waits for them, and re-layouts  1.6 us

profile of v2, /device:TPU:56, one launch (start us, length us, event | category | flops | bytes accessed | tf_op | source)
XLA Modules:
  0.0 39.6 jit_solution(5863578674994111212)
XLA Ops:
  0.0 38.0 %band.1 = f32[384,1920]{1,0:T(8,128)S(1)} custom-call(bf16[384,2048]{1,0:T(8,128)(2,1)} %x_ref.1, s32[3,384]{1,0:T(4,128)} %table_ref.1, s32[3,2048]{1,0:T(4,128)} %gvec_ref.1, f32[4,4096]{1,0:T(4,128)} %bitcast.3, f32[8,4096]{1,0:T(8,128)} %bitcast.2), custom_call_target="tpu_custom_call" | custom-call | tf_op jit(solution)/shard_map/band/pallas_call | solution.py:276
  38.0 1.6 %copy.7 = f32[384,1920]{1,0:T(8,128)} copy(f32[384,1920]{1,0:T(8,128)S(1)} %band.1) | data formatting | bytes 5898240

commit v3 on v2

--- a/solution.py
+++ b/solution.py
@@ -10,8 +10,11 @@
 MESH = pl.DeviceIdType.MESH
 CHUNK = 128
 PIECES = (64, 64, 64, 64, 64, 32, 32)
-FOOT_WAITS = 3
+FOOT_HOLDS = 4
+LIFTED = 4
+DIRECT = 5
 COLUMN = 8
+COLUMNS = 4
 KSTEP = 512
 SCALE_ROWS = 32
 
@@ -32,7 +35,7 @@
 def kernel(
     n, x_ref, table_ref, gvec_ref, val_ref, cond_ref, out_ref,
     both, other, relay, far, far_out, far_in, table, gvec, val, cond, terms, weight, energy,
-    local_sem, sib_sem, block_sem, relay_sem, side_sem, back_sem, helper_ready, foot_ready,
+    local_sem, sib_sem, block_sem, relay_sem, side_sem, back_sem, helper_ready, foot_ready, lift_ready,
 ):
     rows, width = x_ref.shape
     chunks = rows // CHUNK
@@ -52,6 +55,18 @@
     helped_foot = lax.rem(me + 2 * COLUMN - 1, n)
     helped_top = lax.rem(me + 2 * COLUMN - 2, n)
     top_helper = lax.rem(me + n - 2 * COLUMN + 2, n)
+    column = lax.rem(me // (2 * COLUMN), COLUMNS)
+    first_foot = jnp.logical_and(foot, column == 0)
+    last_helper = jnp.logical_and(helper, column == COLUMNS - 1)
+    last_top = jnp.logical_and(top, column == COLUMNS - 1)
+    lifter = jnp.logical_and(
+        jnp.logical_and(level == COLUMN - 1, core == 0), column == 0
+    )
+    apart = 2 * COLUMN * (COLUMNS - 1) + 1
+    my_lifter = lax.rem(me + n - apart, n)
+    foot_lifter = lax.rem(me + n - apart - 1, n)
+    lifted_top = lax.rem(me + apart, n)
+    lifted_foot = lax.rem(me + apart + 1, n)
     at_own = 2 * rows
     at_sib = pl.multiple_of((3 - 2 * core) * rows, 128)
     at_out = pl.multiple_of((1 + 2 * core) * rows, 128)
@@ -78,6 +93,14 @@
     def _():
         signal(barrier, helped_foot)
         signal(barrier, helped_top)
+
+    @pl.when(last_top)
+    def _():
+        signal(barrier, my_lifter)
+
+    @pl.when(first_foot)
+    def _():
+        signal(barrier, foot_lifter)
 
     locals_ = [
         pltpu.make_async_copy(src, dst, local_sem.at[i])
@@ -93,7 +116,7 @@
     ]
     for copy in locals_:
         copy.start()
-    pl.semaphore_wait(barrier, jnp.where(top, 3, 2))
+    pl.semaphore_wait(barrier, jnp.where(lifter, 4, jnp.where(top, 3, 2)))
 
     blocks = [
         remote(x_ref.at[part], other.at[part], block_sem.at[0, i], block_sem.at[1, i], out)
@@ -111,25 +134,54 @@
 
     beside = remote(x_ref, both.at[pl.ds(rows, rows)], sib_sem.at[0], sib_sem.at[1], sib)
 
+    lift = remote(
+        x_ref.at[parts[LIFTED]], relay.at[parts[LIFTED]],
+        block_sem.at[0, LIFTED], relay_sem.at[1, LIFTED], my_lifter,
+    )
+    lift_on = remote(
+        relay.at[parts[LIFTED]], other.at[parts[LIFTED]],
+        relay_sem.at[0, LIFTED], block_sem.at[1, LIFTED], lifted_foot,
+    )
+
+    @pl.when(lifter)
+    def _():
+        signal(lift_ready, lifted_top)
+
     @pl.when(foot)
     def _():
-        for copy in passes:
-            copy.start()
+        for i, copy in enumerate(passes):
+            if i == DIRECT:
+                pl.when(jnp.logical_not(first_foot))(copy.start)
+            else:
+                copy.start()
 
     @pl.when(jnp.logical_not(foot))
     def _():
-        for copy in blocks:
-            copy.start()
+        for i, copy in enumerate(blocks):
+            if i == LIFTED:
+                pl.when(jnp.logical_not(last_top))(copy.start)
+            else:
+                copy.start()
 
     beside.start()
+
+    @pl.when(last_top)
+    def _():
+        pl.semaphore_wait(lift_ready, 1)
+        lift.start()
 
     onward = [
         remote(relay.at[part], other.at[part], relay_sem.at[0, i], block_sem.at[1, i], helped_top)
         for i, part in enumerate(parts)
     ]
 
+    def hands_on(i):
+        if i == DIRECT:
+            return jnp.logical_and(helper, jnp.logical_not(last_helper))
+        return helper
+
     def hand_on(i):
-        @pl.when(helper)
+        @pl.when(hands_on(i))
         def _():
             passes[i].wait_recv()
             onward[i].start()
@@ -191,6 +243,12 @@
 
     lax.fori_loop(0, chunks, own, 0)
 
+    @pl.when(helper)
+    def _():
+        pl.semaphore_wait(helper_ready, 1)
+
+    hand_on(0)
+
     beside.wait_recv()
     scale(both, rows, rows)
 
@@ -203,15 +261,10 @@
 
     lax.fori_loop(0, chunks, near, 0)
 
-    @pl.when(helper)
-    def _():
-        pl.semaphore_wait(helper_ready, 1)
-
     @pl.when(foot)
     def _():
         pl.semaphore_wait(foot_ready, 1)
-
-    hand_on(0)
+        pl.when(first_foot)(blocks[DIRECT].start)
 
     sides, backs, group_rows = [], [], []
     for i, part in enumerate(parts):
@@ -223,9 +276,26 @@
         backs.append(
             remote(far_out.at[part], far_in.at[part], back_sem.at[0, i], back_sem.at[1, i], out)
         )
-        pl.when(jnp.logical_not(foot))(backs[-1].start)
+        if i < FOOT_HOLDS:
+            pl.when(jnp.logical_not(foot))(backs[i].start)
+        else:
+            if i == FOOT_HOLDS:
+
+                @pl.when(foot)
+                def _():
+                    for copy in backs[:FOOT_HOLDS]:
+                        copy.start()
+
+            backs[i].start()
         if i + 1 < len(parts):
             hand_on(i + 1)
+        if i == 1:
+
+            @pl.when(lifter)
+            def _():
+                lift.wait_recv()
+                lift_on.start()
+
         end = part.start + part.size
         if end % CHUNK:
             continue
@@ -248,22 +318,14 @@
     for i, part in enumerate(parts):
         backs[i].wait_recv()
         out_ref[part, pl.ds(at_far, rows)] = far_in[part, :].astype(jnp.float32)
-        if i == FOOT_WAITS:
-
-            @pl.when(foot)
-            def _():
-                for copy in backs:
-                    copy.start()
-
     for copy in sides:
         copy.wait()
     for copy in blocks + backs + [beside]:
         copy.wait_send()
 
-    @pl.when(helper)
-    def _():
-        for copy in onward:
-            copy.wait_send()
+    for i, copy in enumerate(onward):
+        pl.when(hands_on(i))(copy.wait_send)
+    pl.when(lifter)(lift_on.wait_send)
 
 
 def shards(pair_density, table, gvec, val_energy, cond_energy):
@@ -300,6 +362,7 @@
             pltpu.SemaphoreType.DMA((2, len(PIECES))),
             pltpu.SemaphoreType.REGULAR,
             pltpu.SemaphoreType.REGULAR,
+            pltpu.SemaphoreType.REGULAR,
         ],
         compiler_params=pltpu.CompilerParams(
             collective_id=0, has_side_effects=True, vmem_limit_bytes=32 << 20

time: 39.8 us -> 37 us (0.930)
  Pallas kernels: 38 us -> 35.1 us
    pallas_call x1, Pallas kernels: 38 us -> 35.1 us  [shards(): pl.pallas_call(functools.partial(kernel, n), out_shape=jax.ShapeDtypeStru...]
where the time goes in v3:
time: 37 us; the launch traced here: 36.7 us
  Pallas kernels  35.1 us (95%)
  local copies, waits for them, and re-layouts  1.6 us (4%)
    pallas_call x1, Pallas kernels, shards(): pl.pallas_call(functools.partial(kernel, n), out_shape=jax.ShapeDtypeStru...  35.1 us
    unnamed x1, local copies, waits for them, and re-layouts  1.6 us

profile of v3, /device:TPU:56, one launch (start us, length us, event | category | flops | bytes accessed | tf_op | source)
XLA Modules:
  0.0 36.7 jit_solution(4320680240993972064)
XLA Ops:
  0.0 35.1 %band.1 = f32[384,1920]{1,0:T(8,128)S(1)} custom-call(bf16[384,2048]{1,0:T(8,128)(2,1)} %x_ref.1, s32[3,384]{1,0:T(4,128)} %table_ref.1, s32[3,2048]{1,0:T(4,128)} %gvec_ref.1, f32[4,4096]{1,0:T(4,128)} %bitcast.3, f32[8,4096]{1,0:T(8,128)} %bitcast.2), custom_call_target="tpu_custom_call" | custom-call | tf_op jit(solution)/shard_map/band/pallas_call | solution.py:338
  35.1 1.6 %copy.7 = f32[384,1920]{1,0:T(8,128)} copy(f32[384,1920]{1,0:T(8,128)S(1)} %band.1) | data formatting | bytes 5898240

commit v4 on v3

--- a/solution.py
+++ b/solution.py
@@ -10,7 +10,7 @@
 MESH = pl.DeviceIdType.MESH
 CHUNK = 128
 PIECES = (64, 64, 64, 64, 64, 32, 32)
-FOOT_HOLDS = 4
+FOOT_HOLDS = 5
 LIFTED = 4
 DIRECT = 5
 COLUMN = 8
@@ -289,7 +289,7 @@
             backs[i].start()
         if i + 1 < len(parts):
             hand_on(i + 1)
-        if i == 1:
+        if i == 0:
 
             @pl.when(lifter)
             def _():
@@ -315,17 +315,25 @@
             factor * times_transposed(both[pl.ds(0, rows), :], other[chunk, :])
         )
 
-    for i, part in enumerate(parts):
+    def came_back(i):
         backs[i].wait_recv()
-        out_ref[part, pl.ds(at_far, rows)] = far_in[part, :].astype(jnp.float32)
-    for copy in sides:
-        copy.wait()
-    for copy in blocks + backs + [beside]:
+        out_ref[parts[i], pl.ds(at_far, rows)] = far_in[parts[i], :].astype(jnp.float32)
+
+    last = len(parts) - 1
+    for copy in blocks + [beside]:
         copy.wait_send()
-
     for i, copy in enumerate(onward):
         pl.when(hands_on(i))(copy.wait_send)
     pl.when(lifter)(lift_on.wait_send)
+    for i in range(last):
+        came_back(i)
+    for copy in backs[: last - 1]:
+        copy.wait_send()
+    for copy in sides:
+        copy.wait()
+    came_back(last)
+    for copy in backs[last - 1 :]:
+        copy.wait_send()
 
 
 def shards(pair_density, table, gvec, val_energy, cond_energy):

time: 37 us -> 36.9 us (level)
  no operation moved by 1% of the time
where the time goes in v4:
time: 36.9 us; the launch traced here: 36.7 us
  Pallas kernels  35 us (95%)
  local copies, waits for them, and re-layouts  1.6 us (4%)
    pallas_call x1, Pallas kernels, shards(): pl.pallas_call(functools.partial(kernel, n), out_shape=jax.ShapeDtypeStru...  35 us
    unnamed x1, local copies, waits for them, and re-layouts  1.6 us

profile of v4, /device:TPU:56, one launch (start us, length us, event | category | flops | bytes accessed | tf_op | source)
XLA Modules:
  0.0 36.7 jit_solution(11007886018516425629)
XLA Ops:
  0.0 35.0 %band.1 = f32[384,1920]{1,0:T(8,128)S(1)} custom-call(bf16[384,2048]{1,0:T(8,128)(2,1)} %x_ref.1, s32[3,384]{1,0:T(4,128)} %table_ref.1, s32[3,2048]{1,0:T(4,128)} %gvec_ref.1, f32[4,4096]{1,0:T(4,128)} %bitcast.3, f32[8,4096]{1,0:T(8,128)} %bitcast.2), custom_call_target="tpu_custom_call" | custom-call | tf_op jit(solution)/shard_map/band/pallas_call | solution.py:346
  35.1 1.6 %copy.7 = f32[384,1920]{1,0:T(8,128)} copy(f32[384,1920]{1,0:T(8,128)S(1)} %band.1) | data formatting | bytes 5898240

commit v5 on v4

--- a/solution.py
+++ b/solution.py
@@ -15,6 +15,7 @@
 DIRECT = 5
 COLUMN = 8
 COLUMNS = 4
+LIFTER = 1
 KSTEP = 512
 SCALE_ROWS = 32
 
@@ -60,9 +61,9 @@
     last_helper = jnp.logical_and(helper, column == COLUMNS - 1)
     last_top = jnp.logical_and(top, column == COLUMNS - 1)
     lifter = jnp.logical_and(
-        jnp.logical_and(level == COLUMN - 1, core == 0), column == 0
-    )
-    apart = 2 * COLUMN * (COLUMNS - 1) + 1
+        jnp.logical_and(level == COLUMN - 1, core == 0), column == LIFTER
+    )
+    apart = 2 * COLUMN * (COLUMNS - 1 - LIFTER) + 1
     my_lifter = lax.rem(me + n - apart, n)
     foot_lifter = lax.rem(me + n - apart - 1, n)
     lifted_top = lax.rem(me + apart, n)

time: 36.9 us -> 36.9 us (level)
  no operation moved by 1% of the time
where the time goes in v5:
time: 36.9 us; the launch traced here: 36.7 us
  Pallas kernels  35 us (95%)
  local copies, waits for them, and re-layouts  1.6 us (4%)
    pallas_call x1, Pallas kernels, shards(): pl.pallas_call(functools.partial(kernel, n), out_shape=jax.ShapeDtypeStru...  35 us
    unnamed x1, local copies, waits for them, and re-layouts  1.6 us

profile of v5, /device:TPU:56, one launch (start us, length us, event | category | flops | bytes accessed | tf_op | source)
XLA Modules:
  0.0 36.7 jit_solution(13346396976101170895)
XLA Ops:
  0.0 35.0 %band.1 = f32[384,1920]{1,0:T(8,128)S(1)} custom-call(bf16[384,2048]{1,0:T(8,128)(2,1)} %x_ref.1, s32[3,384]{1,0:T(4,128)} %table_ref.1, s32[3,2048]{1,0:T(4,128)} %gvec_ref.1, f32[4,4096]{1,0:T(4,128)} %bitcast.3, f32[8,4096]{1,0:T(8,128)} %bitcast.2), custom_call_target="tpu_custom_call" | custom-call | tf_op jit(solution)/shard_map/band/pallas_call | solution.py:347
  35.1 1.6 %copy.7 = f32[384,1920]{1,0:T(8,128)} copy(f32[384,1920]{1,0:T(8,128)S(1)} %band.1) | data formatting | bytes 5898240
